TPU v7x, 256 devices: a whole 4x4x8 slice. The times are simulated.
256 devices in a mesh: dp: 2 (over x_hi), row: 16 (over z, core), col: 8 (over x_lo, y).
Axes of the slice: x: 4 (x_hi: 2, x_lo: 2; x = x_hi * 2 + x_lo), y: 4, z: 8, core: 2. Of those that a mesh axis runs over, the one named last changes fastest.
Arguments:
- tokens: bfloat16 [2048, 6144], P(('dp', 'col'), 'row'), may hold values from -6 to 6
- w_up: bfloat16 [6144, 24576], P('row', 'col'), may hold values from -0.078125 to 0.078125
- cotangent: bfloat16 [2048, 24576], P(('dp', 'row'), 'col'), may hold values from -6 to 6
Outputs:
- hidden: bfloat16 [2048, 24576], P(('dp', 'row'), 'col')
- weight_grad: float32 [6144, 24576], P('row', ('col', 'dp'))
- input_grad: bfloat16 [2048, 6144], P(('dp', 'col'), 'row')
All inputs are finite; a program needn't handle non-finite values.
Results may differ from a plain program's by a relative error of at most 0.025.
Values may be sent and summed in bfloat16 or wider, within the bound.
No kernel may reach another device: no remote copies, remote signals or barrier semaphores. Data moves between devices by JAX's collectives and lax.ppermute only.
A program may use at most 128 MiB of HBM per device.

v0:
```python
import jax
import jax.numpy as jnp
from jax import lax
from jax.sharding import PartitionSpec as P


def shards(tokens, w_up, cotangent):
    group_rows = tokens.shape[0] * lax.axis_size("col")
    token_panel = lax.all_gather(tokens, "col", axis=0, tiled=True)
    picked = token_panel
    pre_act = lax.psum_scatter(
        jnp.dot(picked, w_up, preferred_element_type=jnp.float32).astype(jnp.bfloat16),
        "row",
        scatter_dimension=0,
        tiled=True,
    ).astype(jnp.float32)
    activated, pullback = jax.vjp(jax.nn.gelu, pre_act)
    hidden = activated.astype(jnp.bfloat16)
    (grad_local,) = pullback(cotangent.astype(jnp.float32))
    grad_full = lax.all_gather(grad_local.astype(jnp.bfloat16), "row", axis=0, tiled=True)
    local_grad = lax.dot_general(
        token_panel, grad_full, (((0,), (0,)), ((), ())), preferred_element_type=jnp.float32
    )
    loss_scale = float(group_rows * lax.axis_size("dp")) ** (-0.5)
    weight_grad = (
        lax.psum_scatter(
            local_grad.astype(jnp.bfloat16), "dp", scatter_dimension=1, tiled=True
        ).astype(jnp.float32)
        * loss_scale
    )
    picked = grad_full
    input_grad = lax.psum_scatter(
        lax.dot_general(
            picked, w_up, (((1,), (1,)), ((), ())), preferred_element_type=jnp.float32
        ).astype(jnp.bfloat16),
        "col",
        scatter_dimension=0,
        tiled=True,
    )
    return (hidden, weight_grad, input_grad)


def solution(mesh):
    placed = (P(("dp", "col"), "row"), P("row", "col"), P(("dp", "row"), "col"))
    return jax.shard_map(
        shards,
        mesh=mesh,
        in_specs=placed,
        out_specs=(P(("dp", "row"), "col"), P("row", ("col", "dp")), P(("dp", "col"), "row")),
        check_vma=False,
    )
```

profile of v0, /device:TPU:4, one launch (start us, length us, event | category | flops | bytes accessed | tf_op | source)
XLA Modules:
  0.0 256.9 jit_solution(833858031628339009)
XLA Ops:
  7.2 0.0 copy-start
  7.2 0.0 reduce-scatter.4.cloned.1.call-start
  7.2 30.3 %all_gather.6 = bf16[1024,384]{1,0:T(8,128)(2,1)S(1)} all-gather(bf16[128,384]{1,0:T(8,128)(2,1)} %param.3), channel_id=1, replica_groups=mesh['dp'=2,'row'=16,'col'=8] {'col'}, dimensions={0}, use_global_device_ids=true | all-gather | bytes 884736 | tf_op jit(solution)/shard_map/all_gather | solution.py:9
  37.5 0.0 copy-done
  37.5 5.4 %convolution_convert_fusion = bf16[1024,3072]{1,0:T(8,128)(2,1)} fusion(bf16[1024,384]{1,0:T(8,128)(2,1)S(1)} %all_gather.6, bf16[384,3072]{1,0:T(8,128)(2,1)S(1)} %copy-done), kind=kOutput, calls=%fused_computation | convolution fusion | flops 2419064832 | bytes 9437184 | tf_op jit(solution)/shard_map/dot_general | solution.py:12
  43.0 0.0 copy-start.1
  43.0 0.0 reduce-scatter.4.cloned.1.call-update
  43.0 0.0 all-gather.2.cloned.1.call-start
  43.0 69.2 %reduce-scatter.4.cloned.1.call-done = bf16[64,3072]{1,0:T(8,128)(2,1)} async-done(((bf16[1024,3072]{1,0:T(8,128)(2,1)}), bf16[64,3072]{1,0:T(8,128)(2,1)}) %reduce-scatter.4.cloned.1.call-update) | async-done | bytes 393232 | tf_op jit(solution)/shard_map/reduce_scatter | solution.py:11
  112.2 0.0 copy-done.1
  112.2 2.5 fusion.4
  114.7 0.0 all-gather.2.cloned.1.call-update
  114.7 0.0 reduce-scatter.6.cloned.1.call-start
  114.8 44.7 %all-gather.2.cloned.1.call-done = bf16[1024,3072]{1,0:T(8,128)(2,1)} async-done(((bf16[64,3072]{1,0:T(8,128)(2,1)}), bf16[1024,3072]{1,0:T(8,128)(2,1)}) %all-gather.2.cloned.1.call-update) | async-done | bytes 6291472 | tf_op jit(solution)/shard_map/all_gather | solution.py:20
  159.5 7.7 %fusion = bf16[384,3072]{0,1:T(8,128)(2,1)} fusion(bf16[1024,3072]{1,0:T(8,128)(2,1)} %all-gather.2.cloned.1.call-done, bf16[1024,384]{1,0:T(8,128)(2,1)S(1)} %all_gather.6), kind=kOutput, calls=%fused_computation.2 | convolution fusion | flops 2417098752 | bytes 9437184 | tf_op jit(solution)/shard_map/dot_general | solution.py:21
  167.1 0.0 reduce-scatter.6.cloned.1.call-update
  167.1 0.0 reduce-scatter.8.cloned.1.call-start
  167.2 6.5 %convolution_convert_fusion.2 = bf16[1024,384]{1,0:T(8,128)(2,1)} fusion(bf16[1024,3072]{1,0:T(8,128)(2,1)} %all-gather.2.cloned.1.call-done, bf16[384,3072]{1,0:T(8,128)(2,1)S(1)} %copy-done), kind=kOutput, calls=%fused_computation.9 | convolution fusion | flops 2416312320 | bytes 9437184 | tf_op jit(solution)/shard_map/dot_general | solution.py:33
  173.7 0.0 reduce-scatter.8.cloned.1.call-update
  173.7 30.8 %reduce-scatter.6.cloned.1.call-done = bf16[384,1536]{0,1:T(8,128)(2,1)} async-done(((bf16[384,3072]{0,1:T(8,128)(2,1)}), bf16[384,1536]{0,1:T(8,128)(2,1)}) %reduce-scatter.6.cloned.1.call-update) | async-done | bytes 1179664 | tf_op jit(solution)/shard_map/reduce_scatter | solution.py:26
  204.5 2.9 %convert_multiply_fusion = f32[384,1536]{0,1:T(8,128)} fusion(bf16[384,1536]{0,1:T(8,128)(2,1)} %reduce-scatter.6.cloned.1.call-done), kind=kLoop, calls=%fused_computation.3 | loop fusion | flops 1179648 | bytes 3538944 | tf_op jit(solution)/shard_map/mul | solution.py:26
  207.4 3.0 %copy.6 = f32[384,1536]{1,0:T(8,128)} copy(f32[384,1536]{0,1:T(8,128)} %convert_multiply_fusion) | data formatting | bytes 4718592
  210.5 39.9 %reduce-scatter.8.cloned.1.call-done = bf16[128,384]{1,0:T(8,128)(2,1)} async-done(((bf16[1024,384]{1,0:T(8,128)(2,1)}), bf16[128,384]{1,0:T(8,128)(2,1)}) %reduce-scatter.8.cloned.1.call-update) | async-done | bytes 98320 | tf_op jit(solution)/shard_map/reduce_scatter | solution.py:32
Async XLA Ops:
  7.2 30.4 %copy-start = (bf16[384,3072]{1,0:T(8,128)(2,1)S(1)}, bf16[384,3072]{1,0:T(8,128)(2,1)}, u32[]{:S(2)}) copy-start(bf16[384,3072]{1,0:T(8,128)(2,1)} %param.4) | copy-start | bytes 7077892
  7.2 105.0 %reduce-scatter.4.cloned.1.call-start = ((), (), s32[]{:S(2)}) async-start(), calls=%async_computation.3 | async-start | bytes 6684672 | tf_op jit(solution)/shard_map/reduce_scatter | solution.py:11
  43.0 69.2 %copy-start.1 = (bf16[64,3072]{1,0:T(8,128)(2,1)S(1)}, bf16[64,3072]{1,0:T(8,128)(2,1)}, u32[]{:S(2)}) copy-start(bf16[64,3072]{1,0:T(8,128)(2,1)} %param.5) | copy-start | bytes 1179652
  43.0 116.5 %all-gather.2.cloned.1.call-start = ((), (), s32[]{:S(2)}) async-start(), calls=%async_computation.4 | async-start | bytes 6684672 | tf_op jit(solution)/shard_map/all_gather | solution.py:20
  114.7 89.8 %reduce-scatter.6.cloned.1.call-start = ((), (), s32[]{:S(2)}) async-start(), calls=%async_computation.5 | async-start | bytes 3538944 | tf_op jit(solution)/shard_map/reduce_scatter | solution.py:26
  167.1 83.2 %reduce-scatter.8.cloned.1.call-start = ((), (), s32[]{:S(2)}) async-start(), calls=%async_computation.6 | async-start | bytes 884736 | tf_op jit(solution)/shard_map/reduce_scatter | solution.py:32
Sparse Core Ops, SparseCore 0:
  43.1 69.0 reduce-scatter.3
  114.8 44.5 all-gather.1
  167.3 37.2 reduce-scatter.5
  207.7 42.6 reduce-scatter.7
where the time goes:
time: 257 us
  waiting for transfers between devices  185 us (72%)
  blocking collectives  30.3 us (12%)
  matrix products  19.6 us (8%)
  between operations  13.8 us (5%)
  other arithmetic  5.37 us (2%)
  local copies, waits for them, and re-layouts  3.06 us (1%)
    reduce_scatter x1, waiting for transfers between devices, shards(): lax.psum_scatter(jnp.dot(picked, w_up, preferred_element_type=jnp.float32...  69.2 us
    all_gather x1, waiting for transfers between devices, shards(): lax.all_gather(grad_local.astype(jnp.bfloat16), 'row', axis=0, tiled=True)  44.7 us
    reduce_scatter x1, waiting for transfers between devices, shards(): lax.psum_scatter(lax.dot_general(picked, w_up, (((1,), (1,)), ((), ())),...  39.9 us
    reduce_scatter x1, waiting for transfers between devices, shards(): lax.psum_scatter(local_grad.astype(jnp.bfloat16), 'dp', scatter_dimension...  30.8 us
    all_gather x1, blocking collectives, shards(): token_panel = lax.all_gather(tokens, 'col', axis=0, tiled=True)  30.3 us
    dot_general x1, matrix products, shards(): lax.dot_general(token_panel, grad_full, (((0,), (0,)), ((), ())), preferr...  7.67 us
    dot_general x1, matrix products, shards(): lax.dot_general(picked, w_up, (((1,), (1,)), ((), ())), preferred_element...  6.5 us
    dot_general x1, matrix products, shards(): jnp.dot(picked, w_up, preferred_element_type=jnp.float32)  5.43 us
  transfers between devices with their start and end apart: 4, of which 4 were waited for; matrix products, arithmetic and copies ran while one was open for 5% of the time, Pallas kernels for 0%

commit v1 on v0

v1 whole, which is shorter than its diff:
```python
import jax
import jax.numpy as jnp
from jax import lax
from jax.sharding import Mesh, PartitionSpec as P

AXES = ("dp", "z", "core", "xl", "y")
SWAP = [(0, 1), (1, 0)]
BF16, F32 = jnp.bfloat16, jnp.float32


def shards(tokens, w_up, cotangent):
    nz, ncol = lax.axis_size("z"), lax.axis_size("xl") * lax.axis_size("y")
    half_z = nz // 2
    d, z, c = (lax.axis_index(name) for name in ("dp", "z", "core"))
    rows, depth = tokens.shape
    part = rows // 2
    cols = w_up.shape[1] // 2
    step = 1 - 2 * c
    ring = [(2 * i, 2 * ((i + 1) % nz)) for i in range(nz)] + [
        (2 * i + 1, 2 * ((i - 1) % nz) + 1) for i in range(nz)
    ]

    def swap(value):
        return lax.ppermute(value, "core", SWAP)

    def along(value):
        return lax.ppermute(value, ("z", "core"), ring)

    def mine(value):
        return lax.dynamic_slice_in_dim(value, c * part, part, 0)

    def theirs(value):
        return lax.dynamic_slice_in_dim(value, (1 - c) * part, part, 0)

    def halves(value):
        return (
            lax.dynamic_slice_in_dim(value, (1 - d) * cols, cols, 1),
            lax.dynamic_slice_in_dim(value, d * cols, cols, 1),
        )

    def dot(a, b, over):
        return lax.dot_general(a, b, (over, ((), ())), preferred_element_type=F32)

    weights = halves(jnp.concatenate([w_up, swap(w_up)], 0))
    own_panel = lax.all_to_all(
        jnp.broadcast_to(tokens[None], (ncol,) + tokens.shape), ("xl", "y"), 0, 0
    ).reshape(ncol * rows, depth)
    panel = jnp.concatenate([own_panel, swap(own_panel)], 1)

    def chunk(hop):
        return lax.dynamic_slice_in_dim(panel, ((z + hop + nz) % nz) * rows, rows, 0)

    own_rows = mine(chunk(0))
    far_rows = mine(chunk(half_z))

    first = along(
        jnp.concatenate([dot(far_rows, w, ((1,), (0,))).astype(BF16) for w in weights], 1)
    )
    owner = (lax.broadcasted_iota(jnp.int32, (rows, 1), 0) // part) == c
    held = [
        jnp.where(owner, jnp.concatenate([f, f], 0), jnp.zeros((), BF16))
        for f in (first[:, :cols], first[:, cols:])
    ]
    for hop in range(half_z - 1, 0, -1):
        x = chunk(step * hop)
        held = [
            along((dot(x, w, ((1,), (0,))) + h.astype(F32)).astype(BF16))
            for w, h in zip(weights, held)
        ]
    hidden, grads = [], []
    for w, h, cot in zip(weights, held, halves(cotangent)):
        pre = (
            dot(own_rows, w, ((1,), (0,)))
            + mine(h).astype(F32)
            + swap(theirs(h)).astype(F32)
        )
        activated, pullback = jax.vjp(jax.nn.gelu, pre)
        hidden.append(activated.astype(BF16))
        (g,) = pullback(cot.astype(F32))
        grads.append(g.astype(BF16))

    blocks = []
    for g in grads:
        other = swap(g)
        held_g = jnp.where(
            c == 0, jnp.concatenate([g, other], 0), jnp.concatenate([other, g], 0)
        )
        got = []
        for _ in range(half_z - 1):
            held_g = along(held_g)
            got.append(held_g)
        blocks.append(got)
    last = [along(mine(got[-1])) for got in blocks]
    blocks = [
        jnp.concatenate(got + [f, g], 0) for got, f, g in zip(blocks, last, grads)
    ]
    x_rows = jnp.concatenate(
        [chunk(-step * hop) for hop in range(1, half_z)] + [far_rows, own_rows], 0
    )

    sums = []
    for g in blocks:
        full = dot(x_rows, g, ((0,), (0,)))
        sums.append(full[:depth] + swap(full[depth:].astype(BF16)).astype(F32))
    sent = lax.ppermute(sums[0].astype(BF16), "dp", SWAP)
    scale = float(nz * rows * lax.axis_size("dp")) ** (-0.5)
    weight_grad = (sums[1] + sent.astype(F32)) * scale

    terms = sum(dot(g, w, ((1,), (1,))) for g, w in zip(blocks, weights)).astype(BF16)
    here, there = terms[:, :depth], swap(terms[:, depth:])
    low = jnp.where(c == 0, here, there)
    high = jnp.where(c == 0, there, here)
    near = (half_z - 1) * rows
    ordered = jnp.concatenate(
        [low[near + part :], high[near + part :], high[:near], low[near : near + part], high[near : near + part]]
        + [low[i * rows : (i + 1) * rows] for i in range(half_z - 2, -1, -1)],
        0,
    )
    twice = jnp.concatenate([ordered, ordered], 0)
    by_col = lax.dynamic_slice_in_dim(twice, ((nz - z) % nz) * rows, nz * rows, 0)
    got = lax.all_to_all(by_col.reshape(ncol, rows, depth), ("xl", "y"), 0, 0)
    input_grad = got.astype(F32).sum(0).astype(BF16)

    hidden = jnp.where(
        d == 0, jnp.concatenate(hidden[::-1], 1), jnp.concatenate(hidden, 1)
    )
    return (hidden, weight_grad, input_grad)


def solution(mesh):
    fine = Mesh(mesh.devices.reshape(2, 8, 2, 2, 4), AXES)
    tokens_at = P(("dp", "xl", "y"), ("z", "core"))
    hidden_at = P(("dp", "z", "core"), ("xl", "y"))
    return jax.shard_map(
        shards,
        mesh=fine,
        in_specs=(tokens_at, P(("z", "core"), ("xl", "y")), hidden_at),
        out_specs=(hidden_at, P(("z", "core"), ("xl", "y", "dp")), tokens_at),
        check_vma=False,
    )
```

time: 257 us -> 178 us (0.69)
  waiting for transfers between devices: 185 us -> 117 us
  blocking collectives: 30.3 us -> 0 us
  starting transfers between devices: 0.16 us -> 15.3 us
  between operations: 13.8 us -> 1.25 us
  local copies, waits for them, and re-layouts: 3.06 us -> 12.8 us
  matrix products: 19.6 us -> 23 us
    reduce_scatter x3 -> x0, waiting for transfers between devices: 140 us -> none  [the longest x1 69.2 us: shards(): lax.psum_scatter(jnp.dot(picked, w_up, preferred_element_type=jnp.float32...]
    ppermute x0 -> x25, waiting for transfers between devices: none -> 73.1 us  [the longest x15 71.9 us: along(): return lax.ppermute(value, ('z', 'core'), ring)]
    all_gather x1 -> x0, waiting for transfers between devices: 44.7 us -> none  [shards(): lax.all_gather(grad_local.astype(jnp.bfloat16), 'row', axis=0, tiled=True)]
    all_to_all x0 -> x2, waiting for transfers between devices: none -> 43.5 us  [the longest x1 30.9 us: shards(): got = lax.all_to_all(by_col.reshape(ncol, rows, depth), ('xl', 'y'), 0, 0)]
    all_gather x1 -> x0, blocking collectives: 30.3 us -> none  [shards(): token_panel = lax.all_gather(tokens, 'col', axis=0, tiled=True)]
    all_to_all x0 -> x2, starting transfers between devices: none -> 9.38 us  [the longest x1 5.1 us: shards(): lax.all_to_all(jnp.broadcast_to(tokens[None], (ncol,) + tokens.shape), ('...]
    ppermute x0 -> x25, starting transfers between devices: none -> 5.91 us  [the longest x15 2.99 us: along(): return lax.ppermute(value, ('z', 'core'), ring)]
    unnamed x5 -> x36, local copies, waits for them, and re-layouts: 3.06 us -> 6.63 us
  transfers between devices with their start and end apart: 4 -> 27, of which waited for: 4 -> 19; matrix products, arithmetic and copies ran while one was open for 5% -> 15% of each run, Pallas kernels for 0% -> 0%
where the time goes in v1:
time: 178 us; the launch traced here: 176 us
  waiting for transfers between devices  117 us (66%)
  matrix products  23 us (13%)
  starting transfers between devices  15.3 us (9%)
  local copies, waits for them, and re-layouts  12.8 us (7%)
  other arithmetic  7.19 us (4%)
    ppermute x15, waiting for transfers between devices, along(): return lax.ppermute(value, ('z', 'core'), ring)  71.9 us
    all_to_all x1, waiting for transfers between devices, shards(): got = lax.all_to_all(by_col.reshape(ncol, rows, depth), ('xl', 'y'), 0, 0)  30.9 us
    dot_general x14, matrix products, dot(): return lax.dot_general(a, b, (over, ((), ())), preferred_element_type=F32)  23 us
    all_to_all x1, waiting for transfers between devices, shards(): lax.all_to_all(jnp.broadcast_to(tokens[None], (ncol,) + tokens.shape), ('...  12.6 us
    unnamed x36, local copies, waits for them, and re-layouts  6.63 us
    all_to_all x1, starting transfers between devices, shards(): lax.all_to_all(jnp.broadcast_to(tokens[None], (ncol,) + tokens.shape), ('...  5.1 us
    all_to_all x1, starting transfers between devices, shards(): got = lax.all_to_all(by_col.reshape(ncol, rows, depth), ('xl', 'y'), 0, 0)  4.27 us
    mul x1, other arithmetic, shards(): weight_grad = (sums[1] + sent.astype(F32)) * scale  3.84 us
  transfers between devices with their start and end apart: 27, of which 19 were waited for; matrix products, arithmetic and copies ran while one was open for 15% of the time, Pallas kernels for 0%

profile of v1, /device:TPU:4, one launch (start us, length us, event | category | flops | bytes accessed | tf_op | source)
XLA Modules:
  0.0 176.2 jit_solution(12896689377660638040)
XLA Ops:
  2.6 5.1 %all-to-all-start = ((bf16[8,128,384]{2,1,0:T(8,128)(2,1)}), bf16[8,128,384]{2,1,0:T(8,128)(2,1)S(1)}, u32[]{:S(2)}, u32[]{:S(2)}) async-start(bf16[8,128,384]{2,1,0:T(8,128)(2,1)} %broadcast_in_dim.22), calls=%async_computation | async-start | bytes 1572864 | tf_op jit(solution)/shard_map/all_to_all | solution.py:45
  7.7 12.6 %all-to-all-done = bf16[8,128,384]{2,1,0:T(8,128)(2,1)S(1)} async-done(((bf16[8,128,384]{2,1,0:T(8,128)(2,1)}), bf16[8,128,384]{2,1,0:T(8,128)(2,1)S(1)}, u32[]{:S(2)}, u32[]{:S(2)}) %all-to-all-start) | async-done | bytes 786464 | tf_op jit(solution)/shard_map/all_to_all | solution.py:45
  28.7 9.7 %collective-permute-done.2 = bf16[64,3072]{1,0:T(8,128)(2,1)S(1)} collective-permute-done((bf16[64,3072]{1,0:T(8,128)(2,1)S(1)}, bf16[64,3072]{1,0:T(8,128)(2,1)S(1)}, u32[]{:S(2)}, u32[]{:S(2)}) %collective-permute-start.2) | collective-permute-done | bytes 393248 | tf_op jit(solution)/shard_map/ppermute | solution.py:27
  38.4 2.3 %fusion.2 = bf16[128,1536]{1,0:T(8,128)(2,1)S(1)} fusion(bf16[768,3072]{1,0:T(8,128)(2,1)} %copy-done, s32[]{:T(128)S(6)} %select_n.147, bf16[64,1536]{1,0:T(8,128)(2,1)S(1)} %get-tuple-element.9, pred[128]{0:T(512)(128)(4,1)S(1)} %fusion.67, s32[]{:T(128)S(6)} %select_n.153, bf16[1024,384]{1,0:T(8,128)(2,1)S(1)} %bitcast.11, ...), kind=kOutput, calls=%fused_computation.24 | convolution fusion | flops 303955968 | bytes 4522120 | tf_op jit(solution)/shard_map/dot_general | solution.py:42
  42.1 7.7 %collective-permute-done.3 = bf16[128,1536]{1,0:T(8,128)(2,1)S(1)} collective-permute-done((bf16[128,1536]{1,0:T(8,128)(2,1)S(1)}, bf16[128,1536]{1,0:T(8,128)(2,1)S(1)}, u32[]{:S(2)}, u32[]{:S(2)}) %collective-permute-start.3) | collective-permute-done | bytes 393248 | tf_op jit(solution)/shard_map/ppermute | solution.py:27
  49.8 2.1 %fusion.1 = bf16[128,1536]{1,0:T(8,128)(2,1)S(1)} fusion(bf16[768,3072]{1,0:T(8,128)(2,1)} %copy-done, s32[]{:T(128)S(6)} %select_n.147, bf16[128,1536]{1,0:T(8,128)(2,1)S(1)} %collective-permute-done.3, s32[]{:T(128)S(6)} %select_n.151, bf16[1024,384]{1,0:T(8,128)(2,1)S(1)} %bitcast.13, bf16[1024,384]{1,0:T(8,128)(2,1)S(1)} %collective-permute-done), kind=kOutput, calls=%fused_computation.23 | convolution fusion | flops 302972928 | bytes 4718600 | tf_op jit(solution)/shard_map/dot_general | solution.py:42
  56.3 4.7 %collective-permute-done.4 = bf16[128,1536]{1,0:T(8,128)(2,1)S(1)} collective-permute-done((bf16[128,1536]{1,0:T(8,128)(2,1)S(1)}, bf16[128,1536]{1,0:T(8,128)(2,1)S(1)}, u32[]{:S(2)}, u32[]{:S(2)}) %collective-permute-start.4) | collective-permute-done | bytes 393248 | tf_op jit(solution)/shard_map/ppermute | solution.py:27
  61.0 2.1 %fusion = bf16[128,1536]{1,0:T(8,128)(2,1)S(1)} fusion(bf16[768,3072]{1,0:T(8,128)(2,1)} %copy-done, s32[]{:T(128)S(6)} %select_n.147, bf16[128,1536]{1,0:T(8,128)(2,1)S(1)} %collective-permute-done.4, s32[]{:T(128)S(6)} %select_n.149, bf16[1024,384]{1,0:T(8,128)(2,1)S(1)} %bitcast.15, bf16[1024,384]{1,0:T(8,128)(2,1)S(1)} %collective-permute-done), kind=kOutput, calls=%fused_computation.22 | convolution fusion | flops 302972928 | bytes 4718600 | tf_op jit(solution)/shard_map/dot_general | solution.py:42
  65.3 2.2 %fusion.3 = bf16[128,1536]{1,0:T(8,128)(2,1)S(1)} fusion(bf16[768,3072]{1,0:T(8,128)(2,1)} %copy-done, s32[]{:T(128)S(6)} %select_n.158, bf16[128,1536]{1,0:T(8,128)(2,1)} %collective-permute-done.8, s32[]{:T(128)S(6)} %select_n.149, bf16[1024,384]{1,0:T(8,128)(2,1)S(1)} %bitcast.16, bf16[1024,384]{1,0:T(8,128)(2,1)S(1)} %collective-permute-done), kind=kOutput, calls=%fused_computation.25 | convolution fusion | flops 302972928 | bytes 4718600 | tf_op jit(solution)/shard_map/dot_general | solution.py:42
  67.6 4.6 %collective-permute-done.5 = bf16[128,1536]{1,0:T(8,128)(2,1)S(1)} collective-permute-done((bf16[128,1536]{1,0:T(8,128)(2,1)S(1)}, bf16[128,1536]{1,0:T(8,128)(2,1)S(1)}, u32[]{:S(2)}, u32[]{:S(2)}) %collective-permute-start.5) | collective-permute-done | bytes 393248 | tf_op jit(solution)/shard_map/ppermute | solution.py:27
  72.4 4.2 %collective-permute-done.9 = bf16[128,1536]{1,0:T(8,128)(2,1)S(1)} collective-permute-done((bf16[128,1536]{1,0:T(8,128)(2,1)S(1)}, bf16[128,1536]{1,0:T(8,128)(2,1)S(1)}, u32[]{:S(2)}, u32[]{:S(2)}) %collective-permute-start.9) | collective-permute-done | bytes 393248 | tf_op jit(solution)/shard_map/ppermute | solution.py:27
  76.9 2.2 %fusion.10 = f32[64,1536]{1,0:T(8,128)S(1)} fusion(bf16[768,3072]{1,0:T(8,128)(2,1)} %copy-done, s32[]{:T(128)S(6)} %select_n.147, bf16[64,1536]{1,0:T(8,128)(2,1)S(1)} %collective-permute-done.6, bf16[128,1536]{1,0:T(8,128)(2,1)S(1)} %collective-permute-done.5, s32[]{:T(128)S(6)} %select_n.142, s32[]{:T(128)S(6)} %dynamic_slice.65, ...), kind=kOutput, calls=%fused_computation.38 | convolution fusion | flops 151584768 | bytes 4718604 | tf_op jit(solution)/shard_map/dot_general | solution.py:42
  79.1 2.6 %fusion.31 = (bf16[64,1536]{1,0:T(8,128)(2,1)S(1)}, bf16[64,1536]{1,0:T(8,128)(2,1)S(1)}, bf16[64,1536]{1,0:T(8,128)(2,1)S(1)}, bf16[64,1536]{1,0:T(8,128)(2,1)S(1)}) fusion(bf16[64,3072]{1,0:T(8,128)(2,1)S(1)} %copy-done.3, s32[]{:T(128)S(6)} %select_n.158, f32[64,1536]{1,0:T(8,128)S(1)} %fusion.10, s32[]{:T(128)S(6)} %select_n.147, ...), kind=kOutput, calls=%fused_computation.70 | convolution fusion | flops 156106752 | bytes 5900800 | tf_op jit(solution)/shard_map/dot_general | solution.py:42
  84.3 8.2 %collective-permute-done.18 = bf16[128,1536]{1,0:T(8,128)(2,1)S(1)} collective-permute-done((bf16[128,1536]{1,0:T(8,128)(2,1)S(1)}, bf16[128,1536]{1,0:T(8,128)(2,1)S(1)}, u32[]{:S(2)}, u32[]{:S(2)}) %collective-permute-start.18) | collective-permute-done | bytes 393248 | tf_op jit(solution)/shard_map/ppermute | solution.py:27
  92.5 4.2 %collective-permute-done.12 = bf16[128,1536]{1,0:T(8,128)(2,1)S(1)} collective-permute-done((bf16[128,1536]{1,0:T(8,128)(2,1)S(1)}, bf16[128,1536]{1,0:T(8,128)(2,1)S(1)}, u32[]{:S(2)}, u32[]{:S(2)}) %collective-permute-start.12) | collective-permute-done | bytes 393248 | tf_op jit(solution)/shard_map/ppermute | solution.py:27
  96.8 4.7 %collective-permute-done.19 = bf16[128,1536]{1,0:T(8,128)(2,1)S(1)} collective-permute-done((bf16[128,1536]{1,0:T(8,128)(2,1)S(1)}, bf16[128,1536]{1,0:T(8,128)(2,1)S(1)}, u32[]{:S(2)}, u32[]{:S(2)}) %collective-permute-start.19) | collective-permute-done | bytes 393248 | tf_op jit(solution)/shard_map/ppermute | solution.py:27
  101.5 4.2 %collective-permute-done.13 = bf16[128,1536]{1,0:T(8,128)(2,1)S(1)} collective-permute-done((bf16[128,1536]{1,0:T(8,128)(2,1)S(1)}, bf16[128,1536]{1,0:T(8,128)(2,1)S(1)}, u32[]{:S(2)}, u32[]{:S(2)}) %collective-permute-start.13) | collective-permute-done | bytes 393248 | tf_op jit(solution)/shard_map/ppermute | solution.py:27
  105.8 4.7 %collective-permute-done.20 = bf16[128,1536]{1,0:T(8,128)(2,1)S(1)} collective-permute-done((bf16[128,1536]{1,0:T(8,128)(2,1)S(1)}, bf16[128,1536]{1,0:T(8,128)(2,1)S(1)}, u32[]{:S(2)}, u32[]{:S(2)}) %collective-permute-start.20) | collective-permute-done | bytes 393248 | tf_op jit(solution)/shard_map/ppermute | solution.py:27
  110.6 4.1 %collective-permute-done.14 = bf16[128,1536]{1,0:T(8,128)(2,1)S(1)} collective-permute-done((bf16[128,1536]{1,0:T(8,128)(2,1)S(1)}, bf16[128,1536]{1,0:T(8,128)(2,1)S(1)}, u32[]{:S(2)}, u32[]{:S(2)}) %collective-permute-start.14) | collective-permute-done | bytes 393248 | tf_op jit(solution)/shard_map/ppermute | solution.py:27
  114.9 2.6 %collective-permute-done.21 = bf16[64,1536]{1,0:T(8,128)(2,1)S(1)} collective-permute-done((bf16[64,1536]{1,0:T(8,128)(2,1)S(1)}, bf16[64,1536]{1,0:T(8,128)(2,1)S(1)}, u32[]{:S(2)}, u32[]{:S(2)}) %collective-permute-start.21) | collective-permute-done | bytes 196640 | tf_op jit(solution)/shard_map/ppermute | solution.py:27
  117.5 4.2 %collective-permute-done.15 = bf16[64,1536]{1,0:T(8,128)(2,1)S(1)} collective-permute-done((bf16[64,1536]{1,0:T(8,128)(2,1)S(1)}, bf16[64,1536]{1,0:T(8,128)(2,1)S(1)}, u32[]{:S(2)}, u32[]{:S(2)}) %collective-permute-start.15) | collective-permute-done | bytes 196640 | tf_op jit(solution)/shard_map/ppermute | solution.py:27
  135.6 4.3 %all-to-all-start.1 = ((bf16[8,128,384]{2,1,0:T(8,128)(2,1)}), bf16[8,128,384]{2,1,0:T(8,128)(2,1)S(1)}, u32[]{:S(2)}, u32[]{:S(2)}) async-start(bf16[8,128,384]{2,1,0:T(8,128)(2,1)} %bitcast.1), calls=%async_computation.1 | async-start | bytes 1572864 | tf_op jit(solution)/shard_map/all_to_all | solution.py:121
  140.7 30.9 %all-to-all-done.1 = bf16[8,128,384]{2,1,0:T(8,128)(2,1)S(1)} async-done(((bf16[8,128,384]{2,1,0:T(8,128)(2,1)}), bf16[8,128,384]{2,1,0:T(8,128)(2,1)S(1)}, u32[]{:S(2)}, u32[]{:S(2)}) %all-to-all-start.1) | async-done | bytes 786464 | tf_op jit(solution)/shard_map/all_to_all | solution.py:121
  172.3 3.8 %fusion.8 = f32[384,1536]{1,0:T(8,128)} fusion(f32[768,1536]{1,0:T(8,128)} %copy-done.2, bf16[384,1536]{1,0:T(8,128)(2,1)} %collective-permute-done.23, bf16[384,1536]{1,0:T(8,128)(2,1)S(1)} %collective-permute-done.16), kind=kLoop, calls=%fused_computation.34 | loop fusion | flops 2949120 | bytes 7077888 | tf_op jit(solution)/shard_map/mul | solution.py:107
  (109 shorter events, 36.7 us)
Async XLA Ops:
  0.6 21.5 %collective-permute-start.1 = (bf16[384,3072]{1,0:T(8,128)(2,1)}, bf16[384,3072]{1,0:T(8,128)(2,1)}, u32[]{:S(2)}, u32[]{:S(2)}) collective-permute-start(bf16[384,3072]{1,0:T(8,128)(2,1)} %param.4), channel_id=1, source_target_pairs={{0,8},{8,0},{1,9},{9,1},{2,10},{10,2},{3,11},{11,3},{4,12},{12,4},... | collective-permute-start | bytes 7077896 | tf_op jit(solution)/shard_map/ppermute | solution.py:24
  2.6 17.8 %all-to-all-start = ((bf16[8,128,384]{2,1,0:T(8,128)(2,1)}), bf16[8,128,384]{2,1,0:T(8,128)(2,1)S(1)}, u32[]{:S(2)}, u32[]{:S(2)}) async-start(bf16[8,128,384]{2,1,0:T(8,128)(2,1)} %broadcast_in_dim.22), calls=%async_computation | async-start | bytes 1572864 | tf_op jit(solution)/shard_map/all_to_all | solution.py:45
  20.3 3.7 %collective-permute-start = (bf16[1024,384]{1,0:T(8,128)(2,1)S(1)}, bf16[1024,384]{1,0:T(8,128)(2,1)S(1)}, u32[]{:S(2)}, u32[]{:S(2)}) collective-permute-start(bf16[1024,384]{1,0:T(8,128)(2,1)S(1)} %bitcast.8), channel_id=1, source_target_pairs={{0,8},{8,0},{1,9},{9,1},{2,10},{10,2},{3,11},{11,3},{4,12},{12,4},... | collective-permute-start | bytes 2359304 | tf_op jit(solution)/shard_map/ppermute | solution.py:24
  26.7 11.7 %collective-permute-start.2 = (bf16[64,3072]{1,0:T(8,128)(2,1)S(1)}, bf16[64,3072]{1,0:T(8,128)(2,1)S(1)}, u32[]{:S(2)}, u32[]{:S(2)}) collective-permute-start(bf16[64,3072]{1,0:T(8,128)(2,1)S(1)} %pad_maximum_fusion), channel_id=1, source_target_pairs={{0,16},{16,32},{32,48},{48,64},{64,80},{80,96},{96,112},{112,0},{8... | collective-permute-start | bytes 1179656 | tf_op jit(solution)/shard_map/ppermute | solution.py:27
  40.7 9.1 %collective-permute-start.3 = (bf16[128,1536]{1,0:T(8,128)(2,1)S(1)}, bf16[128,1536]{1,0:T(8,128)(2,1)S(1)}, u32[]{:S(2)}, u32[]{:S(2)}) collective-permute-start(bf16[128,1536]{1,0:T(8,128)(2,1)S(1)} %fusion.2), channel_id=1, source_target_pairs={{0,16},{16,32},{32,48},{48,64},{64,80},{80,96},{96,112},{112,0},{8... | collective-permute-start | bytes 1179656 | tf_op jit(solution)/shard_map/ppermute | solution.py:27
  42.0 12.1 %collective-permute-start.7 = (bf16[128,1536]{1,0:T(8,128)(2,1)S(1)}, bf16[128,1536]{1,0:T(8,128)(2,1)S(1)}, u32[]{:S(2)}, u32[]{:S(2)}) collective-permute-start(bf16[128,1536]{1,0:T(8,128)(2,1)S(1)} %fusion.5), channel_id=1, source_target_pairs={{0,16},{16,32},{32,48},{48,64},{64,80},{80,96},{96,112},{112,0},{8... | collective-permute-start | bytes 1179656 | tf_op jit(solution)/shard_map/ppermute | solution.py:27
  52.0 9.1 %collective-permute-start.4 = (bf16[128,1536]{1,0:T(8,128)(2,1)S(1)}, bf16[128,1536]{1,0:T(8,128)(2,1)S(1)}, u32[]{:S(2)}, u32[]{:S(2)}) collective-permute-start(bf16[128,1536]{1,0:T(8,128)(2,1)S(1)} %fusion.1), channel_id=1, source_target_pairs={{0,16},{16,32},{32,48},{48,64},{64,80},{80,96},{96,112},{112,0},{8... | collective-permute-start | bytes 1179656 | tf_op jit(solution)/shard_map/ppermute | solution.py:27
  56.2 9.2 %collective-permute-start.8 = (bf16[128,1536]{1,0:T(8,128)(2,1)S(1)}, bf16[128,1536]{1,0:T(8,128)(2,1)}, u32[]{:S(2)}, u32[]{:S(2)}) collective-permute-start(bf16[128,1536]{1,0:T(8,128)(2,1)S(1)} %fusion.4), channel_id=1, source_target_pairs={{0,16},{16,32},{32,48},{48,64},{64,80},{80,96},{96,112},{112,0},{8... | collective-permute-start | bytes 1179656 | tf_op jit(solution)/shard_map/ppermute | solution.py:27
  63.2 9.1 %collective-permute-start.5 = (bf16[128,1536]{1,0:T(8,128)(2,1)S(1)}, bf16[128,1536]{1,0:T(8,128)(2,1)S(1)}, u32[]{:S(2)}, u32[]{:S(2)}) collective-permute-start(bf16[128,1536]{1,0:T(8,128)(2,1)S(1)} %fusion), channel_id=1, source_target_pairs={{0,16},{16,32},{32,48},{48,64},{64,80},{80,96},{96,112},{112,0},{8... | collective-permute-start | bytes 1179656 | tf_op jit(solution)/shard_map/ppermute | solution.py:27
  67.5 9.1 %collective-permute-start.9 = (bf16[128,1536]{1,0:T(8,128)(2,1)S(1)}, bf16[128,1536]{1,0:T(8,128)(2,1)S(1)}, u32[]{:S(2)}, u32[]{:S(2)}) collective-permute-start(bf16[128,1536]{1,0:T(8,128)(2,1)S(1)} %fusion.3), channel_id=1, source_target_pairs={{0,16},{16,32},{32,48},{48,64},{64,80},{80,96},{96,112},{112,0},{8... | collective-permute-start | bytes 1179656 | tf_op jit(solution)/shard_map/ppermute | solution.py:27
  72.3 4.7 %collective-permute-start.6 = (bf16[64,1536]{1,0:T(8,128)(2,1)S(1)}, bf16[64,1536]{1,0:T(8,128)(2,1)S(1)}, u32[]{:S(2)}, u32[]{:S(2)}) collective-permute-start(bf16[64,1536]{1,0:T(8,128)(2,1)S(1)} %constant_dynamic-slice_fusion.4), channel_id=1, source_target_pairs={{0,8},{8,0},{1,9},{9,1},{2,10},{10,2},{3,11},{11,3},{4,12},{12,4},... | collective-permute-start | bytes 589832 | tf_op jit(solution)/shard_map/ppermute | solution.py:24
  83.5 9.1 %collective-permute-start.18 = (bf16[128,1536]{1,0:T(8,128)(2,1)S(1)}, bf16[128,1536]{1,0:T(8,128)(2,1)S(1)}, u32[]{:S(2)}, u32[]{:S(2)}) collective-permute-start(bf16[128,1536]{1,0:T(8,128)(2,1)S(1)} %maximum_select_fusion.4), channel_id=1, source_target_pairs={{0,16},{16,32},{32,48},{48,64},{64,80},{80,96},{96,112},{112,0},{8... | collective-permute-start | bytes 1179656 | tf_op jit(solution)/shard_map/ppermute | solution.py:27
  83.9 12.8 %collective-permute-start.12 = (bf16[128,1536]{1,0:T(8,128)(2,1)S(1)}, bf16[128,1536]{1,0:T(8,128)(2,1)S(1)}, u32[]{:S(2)}, u32[]{:S(2)}) collective-permute-start(bf16[128,1536]{1,0:T(8,128)(2,1)S(1)} %maximum_select_fusion.3), channel_id=1, source_target_pairs={{0,16},{16,32},{32,48},{48,64},{64,80},{80,96},{96,112},{112,0},{8... | collective-permute-start | bytes 1179656 | tf_op jit(solution)/shard_map/ppermute | solution.py:27
  92.5 9.0 %collective-permute-start.19 = (bf16[128,1536]{1,0:T(8,128)(2,1)S(1)}, bf16[128,1536]{1,0:T(8,128)(2,1)S(1)}, u32[]{:S(2)}, u32[]{:S(2)}) collective-permute-start(bf16[128,1536]{1,0:T(8,128)(2,1)S(1)} %collective-permute-done.18), channel_id=1, source_target_pairs={{0,16},{16,32},{32,48},{48,64},{64,80},{80,96},{96,112},{112,0},{8... | collective-permute-start | bytes 1179656 | tf_op jit(solution)/shard_map/ppermute | solution.py:27
  96.7 9.0 %collective-permute-start.13 = (bf16[128,1536]{1,0:T(8,128)(2,1)S(1)}, bf16[128,1536]{1,0:T(8,128)(2,1)S(1)}, u32[]{:S(2)}, u32[]{:S(2)}) collective-permute-start(bf16[128,1536]{1,0:T(8,128)(2,1)S(1)} %collective-permute-done.12), channel_id=1, source_target_pairs={{0,16},{16,32},{32,48},{48,64},{64,80},{80,96},{96,112},{112,0},{8... | collective-permute-start | bytes 1179656 | tf_op jit(solution)/shard_map/ppermute | solution.py:27
  101.5 9.0 %collective-permute-start.20 = (bf16[128,1536]{1,0:T(8,128)(2,1)S(1)}, bf16[128,1536]{1,0:T(8,128)(2,1)S(1)}, u32[]{:S(2)}, u32[]{:S(2)}) collective-permute-start(bf16[128,1536]{1,0:T(8,128)(2,1)S(1)} %collective-permute-done.19), channel_id=1, source_target_pairs={{0,16},{16,32},{32,48},{48,64},{64,80},{80,96},{96,112},{112,0},{8... | collective-permute-start | bytes 1179656 | tf_op jit(solution)/shard_map/ppermute | solution.py:27
  105.7 9.0 %collective-permute-start.14 = (bf16[128,1536]{1,0:T(8,128)(2,1)S(1)}, bf16[128,1536]{1,0:T(8,128)(2,1)S(1)}, u32[]{:S(2)}, u32[]{:S(2)}) collective-permute-start(bf16[128,1536]{1,0:T(8,128)(2,1)S(1)} %collective-permute-done.13), channel_id=1, source_target_pairs={{0,16},{16,32},{32,48},{48,64},{64,80},{80,96},{96,112},{112,0},{8... | collective-permute-start | bytes 1179656 | tf_op jit(solution)/shard_map/ppermute | solution.py:27
  110.5 7.0 %collective-permute-start.21 = (bf16[64,1536]{1,0:T(8,128)(2,1)S(1)}, bf16[64,1536]{1,0:T(8,128)(2,1)S(1)}, u32[]{:S(2)}, u32[]{:S(2)}) collective-permute-start(bf16[64,1536]{1,0:T(8,128)(2,1)S(1)} %constant_dynamic-slice_fusion.1), channel_id=1, source_target_pairs={{0,16},{16,32},{32,48},{48,64},{64,80},{80,96},{96,112},{112,0},{8... | collective-permute-start | bytes 589832 | tf_op jit(solution)/shard_map/ppermute | solution.py:27
  114.7 7.0 %collective-permute-start.15 = (bf16[64,1536]{1,0:T(8,128)(2,1)S(1)}, bf16[64,1536]{1,0:T(8,128)(2,1)S(1)}, u32[]{:S(2)}, u32[]{:S(2)}) collective-permute-start(bf16[64,1536]{1,0:T(8,128)(2,1)S(1)} %constant_dynamic-slice_fusion.2), channel_id=1, source_target_pairs={{0,16},{16,32},{32,48},{48,64},{64,80},{80,96},{96,112},{112,0},{8... | collective-permute-start | bytes 589832 | tf_op jit(solution)/shard_map/ppermute | solution.py:27
  124.7 7.2 %collective-permute-start.24 = (bf16[512,384]{1,0:T(8,128)(2,1)S(1)}, bf16[512,384]{1,0:T(8,128)(2,1)S(1)}, u32[]{:S(2)}, u32[]{:S(2)}) collective-permute-start(bf16[512,384]{1,0:T(8,128)(2,1)S(1)} %slice.73), channel_id=1, source_target_pairs={{0,8},{8,0},{1,9},{9,1},{2,10},{10,2},{3,11},{11,3},{4,12},{12,4},... | collective-permute-start | bytes 1179656 | tf_op jit(solution)/shard_map/ppermute | solution.py:24
  126.6 5.8 %collective-permute-start.22 = (bf16[384,1536]{1,0:T(8,128)(2,1)S(1)}, bf16[384,1536]{1,0:T(8,128)(2,1)S(1)}, u32[]{:S(2)}, u32[]{:S(2)}) collective-permute-start(bf16[384,1536]{1,0:T(8,128)(2,1)S(1)} %slice.110), channel_id=1, source_target_pairs={{0,8},{8,0},{1,9},{9,1},{2,10},{10,2},{3,11},{11,3},{4,12},{12,4},... | collective-permute-start | bytes 3538952 | tf_op jit(solution)/shard_map/ppermute | solution.py:24
  131.9 40.5 %collective-permute-start.16 = (bf16[384,1536]{1,0:T(8,128)(2,1)}, bf16[384,1536]{1,0:T(8,128)(2,1)S(1)}, u32[]{:S(2)}, u32[]{:S(2)}) collective-permute-start(bf16[384,1536]{1,0:T(8,128)(2,1)} %slice.111), channel_id=1, source_target_pairs={{0,8},{8,0},{1,9},{9,1},{2,10},{10,2},{3,11},{11,3},{4,12},{12,4},... | collective-permute-start | bytes 3538952 | tf_op jit(solution)/shard_map/ppermute | solution.py:24
  133.7 38.6 %collective-permute-start.23 = (bf16[384,1536]{1,0:T(8,128)(2,1)}, bf16[384,1536]{1,0:T(8,128)(2,1)}, u32[]{:S(2)}, u32[]{:S(2)}) collective-permute-start(bf16[384,1536]{1,0:T(8,128)(2,1)} %fusion.6), channel_id=1, source_target_pairs={{0,128},{128,0},{1,129},{129,1},{2,130},{130,2},{3,131},{131,3},{4... | collective-permute-start | bytes 3538952 | tf_op jit(solution)/shard_map/ppermute | solution.py:105
  135.6 36.0 %all-to-all-start.1 = ((bf16[8,128,384]{2,1,0:T(8,128)(2,1)}), bf16[8,128,384]{2,1,0:T(8,128)(2,1)S(1)}, u32[]{:S(2)}, u32[]{:S(2)}) async-start(bf16[8,128,384]{2,1,0:T(8,128)(2,1)} %bitcast.1), calls=%async_computation.1 | async-start | bytes 1572864 | tf_op jit(solution)/shard_map/all_to_all | solution.py:121
  (9 other events, 90.9 us)
